TPU v7x, 32 devices: a whole 2x2x4 slice. The times are simulated.
32 devices in a mesh: section: 2 (over x), dp: 8 (over z, core), seq: 2 (over y).
Axes of the slice: x: 2, y: 2, z: 4, core: 2. Of those that a mesh axis runs over, the one named last changes fastest.
Arguments:
- section_input: bfloat16 [2, 2048, 5120], P('section', 'seq', 'dp'), as said below
- norm_gain: bfloat16 [2, 5120], P('section', 'dp'), may hold values from 0.5 to 2
- qkv_weight: bfloat16 [2, 5120, 3072], P('section', 'seq', 'dp'), as said below
- out_weight: bfloat16 [2, 1024, 5120], P('section', None, 'dp'), may hold values from -1 to 1
- random_blocks: int32 [2, 32, 3], P('section', 'seq'), may hold values from 0 to 31
- global_blocks: int32 [2, 2], P('section'), may hold values from 0 to 31, as said below
Outputs:
- handed_on: bfloat16 [2, 2048, 5120], P('section', 'seq', 'dp')
Inputs may be any that keep to these rules, and one draw needn't show every extreme that they name: `section_input`: real values, each token row and each feature column with its own scale. `qkv_weight`: real values of projections. `global_blocks`: 2 different block numbers for each section; the last section's document has the first and the last block as its global blocks.
All inputs are finite; a program needn't handle non-finite values.
Results may differ from a plain program's by a relative error of at most 0.0058.
Values may be sent and summed in bfloat16 or wider, within the bound.
A program may use at most 64 MiB of HBM per device.

v0:
```python
import math

import jax
import jax.numpy as jnp
from jax import lax
from jax.sharding import PartitionSpec as P

BLOCK = 64


def shifted(block, axis, distance):
    devices = range(lax.axis_size(axis))
    route = [((i - distance) % len(devices), i) for i in devices]
    return lax.ppermute(block, axis, route)


def block_mask(query_ids, random_rows, global_ids, key_count):
    query_col = query_ids[:, None]
    key_ids = jnp.arange(key_count, dtype=jnp.int32)[None, :]
    adjacent = jnp.abs(query_col - key_ids) <= 1
    key_global = jnp.any(key_ids[:, :, None] == global_ids[None, None, :], axis=2)
    query_global = jnp.any(query_col[:, :, None] == global_ids[None, None, :], axis=2)
    chosen = jnp.any(random_rows[:, None, :] == key_ids[:, :, None], axis=2)
    return adjacent | key_global | query_global | chosen


def sparse_attention(query, keys, values, allowed, block_size):
    scores = lax.dot_general(
        query, keys, (((1,), (1,)), ((), ())), preferred_element_type=jnp.float32
    )
    scores = scores * (1.0 / math.sqrt(query.shape[1]))
    query_blocks, key_blocks = allowed.shape
    scores = scores.reshape(query_blocks, block_size, key_blocks, block_size)
    live = allowed[:, None, :, None]
    scores = jnp.where(live, scores, -1e30)
    highest = jnp.max(scores, axis=(2, 3), keepdims=True)
    weights = jnp.where(live, jnp.exp(scores - highest), 0.0)
    totals = jnp.sum(weights, axis=(2, 3), keepdims=True)
    probs = (
        (weights / totals)
        .reshape(query_blocks * block_size, key_blocks * block_size)
        .astype(jnp.bfloat16)
    )
    return jnp.dot(probs, values, preferred_element_type=jnp.float32).astype(jnp.bfloat16)


def shards(section_input, norm_gain, qkv_weight, out_weight, random_blocks, global_blocks):
    token_rows = section_input[0]
    token_count = token_rows.shape[0]
    width = norm_gain.shape[1] * lax.axis_size("dp")
    as_float = token_rows.astype(jnp.float32)
    local_squares = jnp.sum(as_float * as_float, axis=1)
    total_squares = lax.psum(local_squares, "dp")
    factor = lax.rsqrt(total_squares / width + 1e-05)[:, None]
    normed_part = (as_float * factor * norm_gain[0].astype(jnp.float32)).astype(jnp.bfloat16)
    normed = lax.all_gather(normed_part, "dp", axis=1, tiled=True)
    weight_half = qkv_weight[0]
    joined = jnp.dot(
        normed,
        lax.all_gather(weight_half, "seq", axis=0, tiled=True),
        preferred_element_type=jnp.float32,
    )
    head_size = joined.shape[1] // 3
    query = joined[:, :head_size].astype(jnp.bfloat16)
    keys_values = joined[:, head_size:].astype(jnp.bfloat16)
    document_kv = lax.all_gather(keys_values, "seq", axis=0, tiled=True)
    keys = document_kv[:, :head_size]
    values = document_kv[:, head_size:]
    own_blocks = token_count // BLOCK
    query_ids = lax.axis_index("seq") * own_blocks + jnp.arange(own_blocks, dtype=jnp.int32)
    allowed = block_mask(
        query_ids, random_blocks[0], global_blocks[0], document_kv.shape[0] // BLOCK
    )
    attended = sparse_attention(query, keys, values, allowed, BLOCK)
    out_columns = out_weight[0]
    added = jnp.dot(
        lax.all_gather(attended, "dp", axis=1, tiled=True),
        out_columns,
        preferred_element_type=jnp.float32,
    )
    result = (token_rows.astype(jnp.float32) + added).astype(jnp.bfloat16)
    return shifted(result[None], "section", 1)


def solution(mesh):
    placed = (
        P("section", "seq", "dp"),
        P("section", "dp"),
        P("section", "seq", "dp"),
        P("section", None, "dp"),
        P("section", "seq", None),
        P("section", None),
    )
    return jax.shard_map(
        shards, mesh=mesh, in_specs=placed, out_specs=P("section", "seq", "dp"), check_vma=False
    )
```

profile of v0, /device:TPU:1, one launch (start us, length us, event | category | flops | bytes accessed | tf_op | source)
XLA Modules:
  0.0 279.8 jit_solution(2408644222850474713)
XLA Ops:
  6.5 0.0 copy-start
  6.5 0.0 copy-start.1
  6.5 0.0 copy-start.4
  6.5 0.0 all-gather.12.cloned.1.call-start
  6.5 0.7 all-gather.12.cloned.1.call-update
  7.3 0.0 all-gather.6.cloned.1.call-start
  7.3 0.6 copy-done.1
  8.0 0.3 fusion.5
  8.3 14.6 %psum.7 = f32[1024]{0:T(1024)S(1)} all-reduce(f32[1024]{0:T(1024)S(1)} %fusion.5), channel_id=1, replica_groups=mesh['section'=2,'dp'=8,'seq'=2] {'dp'}, use_global_device_ids=true, to_apply=%region_4.0 | all-reduce | flops 1024 | bytes 8192 | tf_op jit(solution)/shard_map/psum | solution.py:53
  22.9 0.0 copy-done.4
  23.0 1.4 fusion.7
  24.4 0.0 all-gather.6.cloned.1.call-update
  24.4 0.0 copy-start.5
  24.4 0.0 copy-start.6
  24.4 0.0 all-gather.8.cloned.1.call-start
  24.5 40.3 %all-gather.12.cloned.1.call-done = bf16[1,5120,384]{2,1,0:T(8,128)(2,1)} async-done(((bf16[1,2560,384]{2,1,0:T(8,128)(2,1)}), bf16[1,5120,384]{2,1,0:T(8,128)(2,1)}) %all-gather.12.cloned.1.call-update) | async-done | bytes 3932176 | tf_op jit(solution)/shard_map/all_gather | solution.py:60
  64.8 101.4 %all-gather.6.cloned.1.call-done = bf16[1024,5120]{1,0:T(8,128)(2,1)} async-done(((bf16[1024,640]{1,0:T(8,128)(2,1)}), bf16[1024,5120]{1,0:T(8,128)(2,1)}) %all-gather.6.cloned.1.call-update) | async-done | bytes 10485776 | tf_op jit(solution)/shard_map/all_gather | solution.py:56
  166.2 9.4 %fusion.10 = bf16[1024,384]{1,0:T(8,128)(2,1)S(1)} fusion(bf16[1024,5120]{1,0:T(8,128)(2,1)} %all-gather.6.cloned.1.call-done, bf16[1,5120,384]{2,1,0:T(8,128)(2,1)} %all-gather.12.cloned.1.call-done), kind=kOutput, calls=%fused_computation.16 | convolution fusion | flops 4026925056 | bytes 15204352 | tf_op jit(solution)/shard_map/dot_general | solution.py:58
  175.7 0.0 copy-start.2
  175.7 0.9 copy-done.2
  176.6 0.8 slice.19
  177.4 0.0 all-gather.8.cloned.1.call-update
  177.4 0.2 all-gather.10.cloned.1.call-start
  177.7 0.0 copy-done.5
  177.7 0.0 copy-done.6
  177.7 0.1 compare_reduce_fusion.1
  177.8 0.1 compare_reduce_fusion
  177.9 0.1 fusion.19
  178.0 0.1 fusion.22
  178.0 3.1 %broadcast_in_dim.30 = pred[16,64,32,64]{3,2,1,0:T(32,128)(4,1)} broadcast(pred[16,32]{1,0:T(8,128)(4,1)S(1)} %fusion.22), dimensions={0,2} | broadcast | bytes 2097664 | tf_op jit(solution)/shard_map/jit(_where)/broadcast_in_dim | solution.py:37
  181.1 11.1 %broadcast_in_dim.31 = pred[1024,2048]{1,0:T(32,128)(4,1)S(1)} reshape(pred[16,64,32,64]{3,2,1,0:T(32,128)(4,1)} %broadcast_in_dim.30) | data formatting | bytes 4194304 | tf_op jit(solution)/shard_map/jit(_where)/broadcast_in_dim | solution.py:37
  192.3 4.6 %all-gather.8.cloned.1.call-done = bf16[2048,256]{1,0:T(8,128)(2,1)} async-done(((bf16[1024,256]{1,0:T(8,128)(2,1)}), bf16[2048,256]{1,0:T(8,128)(2,1)}) %all-gather.8.cloned.1.call-update) | async-done | bytes 1048592 | tf_op jit(solution)/shard_map/all_gather | solution.py:66
  196.9 3.1 %fusion = (f32[1024]{0:T(1024)S(1)}, f32[1024,2048]{1,0:T(8,128)S(1)}) fusion(pred[1024,2048]{1,0:T(32,128)(4,1)S(1)} %broadcast_in_dim.31, bf16[2048,256]{1,0:T(8,128)(2,1)} %all-gather.8.cloned.1.call-done, bf16[1024,384]{1,0:T(8,128)(2,1)} %copy-done.2), kind=kOutput, calls=%fused_computation.3 | convolution fusion | flops 543161344 | bytes 11276288 | tf_op jit(solution)/shard_map/dot_general | solution.py:28
  199.9 0.0 copy-start.3
  199.9 3.0 %fusion.1 = f32[1024]{0:T(1024)S(1)} fusion(pred[1024,2048]{1,0:T(32,128)(4,1)S(1)} %broadcast_in_dim.31, f32[1024,2048]{1,0:T(8,128)S(1)} %get-tuple-element.6, f32[1024]{0:T(1024)S(1)} %get-tuple-element.5), kind=kLoop, calls=%fused_computation.4 | loop fusion | flops 10484736 | bytes 10493952 | tf_op jit(solution)/shard_map/reduce_sum | solution.py:38
  203.0 0.0 copy-done.3
  203.0 3.9 %fusion.14 = bf16[1024,128]{1,0:T(8,128)(2,1)} fusion(pred[1024,2048]{1,0:T(32,128)(4,1)S(1)} %broadcast_in_dim.31, f32[1024,2048]{1,0:T(8,128)S(1)} %get-tuple-element.6, f32[1024]{0:T(1024)S(1)} %fusion.1, f32[1024]{0:T(1024)S(1)} %get-tuple-element.5, bf16[2048,256]{1,0:T(8,128)(2,1)S(1)} %copy-done.3), kind=kOutput, calls=%fused_computation.18 | convolution fusion | flops 549584896 | bytes 11280384 | tf_op jit(solution)/shard_map/dot_general | solution.py:44
  206.9 0.0 all-gather.10.cloned.1.call-update
  206.9 31.4 %all-gather.10.cloned.1.call-done = bf16[1024,1024]{1,0:T(8,128)(2,1)} async-done(((bf16[1024,128]{1,0:T(8,128)(2,1)}), bf16[1024,1024]{1,0:T(8,128)(2,1)}) %all-gather.10.cloned.1.call-update) | async-done | bytes 2097168 | tf_op jit(solution)/shard_map/all_gather | solution.py:77
  238.3 0.0 copy-done
  238.3 3.7 %fusion.9 = bf16[1,1024,640]{2,1,0:T(8,128)(2,1)S(1)} fusion(bf16[1024,1024]{1,0:T(8,128)(2,1)} %all-gather.10.cloned.1.call-done, bf16[1,1024,640]{2,1,0:T(8,128)(2,1)S(1)} %copy-done, bf16[1,1024,640]{2,1,0:T(8,128)(2,1)} %param.6), kind=kOutput, calls=%fused_computation.15 | convolution fusion | flops 1344143360 | bytes 6029312 | tf_op jit(solution)/shard_map/dot_general | solution.py:76
  242.0 1.0 collective-permute-start
  243.0 29.2 %collective-permute-done = bf16[1,1024,640]{2,1,0:T(8,128)(2,1)S(1)} collective-permute-done((bf16[1,1024,640]{2,1,0:T(8,128)(2,1)S(1)}, bf16[1,1024,640]{2,1,0:T(8,128)(2,1)S(1)}, u32[]{:S(2)}, u32[]{:S(2)}) %collective-permute-start) | collective-permute-done | bytes 1310752 | tf_op jit(solution)/shard_map/ppermute | solution.py:14
  272.2 1.1 copy.15
  (4 shorter events, 0.0 us)
Async XLA Ops:
  6.5 231.8 %copy-start = (bf16[1,1024,640]{2,1,0:T(8,128)(2,1)S(1)}, bf16[1,1024,640]{2,1,0:T(8,128)(2,1)}, u32[]{:S(2)}) copy-start(bf16[1,1024,640]{2,1,0:T(8,128)(2,1)} %param.9) | copy-start | bytes 3932164
  6.5 1.4 copy-start.1
  6.5 16.4 %copy-start.4 = (bf16[1,640]{1,0:T(2,128)(2,1)S(1)}, bf16[1,640]{1,0:T(2,128)(2,1)}, u32[]{:S(2)}) copy-start(bf16[1,640]{1,0:T(2,128)(2,1)} %param.7) | copy-start | bytes 3844
  6.5 58.3 %all-gather.12.cloned.1.call-start = ((), (), s32[]{:S(2)}) async-start(), calls=%async_computation.3 | async-start | bytes 5898240 | tf_op jit(solution)/shard_map/all_gather | solution.py:60
  7.3 159.0 %all-gather.6.cloned.1.call-start = ((), (), s32[]{:S(2)}) async-start(), calls=%async_computation | async-start | bytes 11796480 | tf_op jit(solution)/shard_map/all_gather | solution.py:56
  24.4 153.3 %copy-start.5 = (s32[1,16,3]{1,0,2:T(1,128)S(1)}, s32[1,16,3]{1,0,2:T(1,128)}, u32[]{:S(2)}) copy-start(s32[1,16,3]{1,0,2:T(1,128)} %param.10) | copy-start | bytes 580
  24.4 153.3 %copy-start.6 = (s32[1,2]{1,0:T(1,128)S(1)}, s32[1,2]{1,0:T(1,128)}, u32[]{:S(2)}) copy-start(s32[1,2]{1,0:T(1,128)} %param.11) | copy-start | bytes 28
  24.4 172.4 %all-gather.8.cloned.1.call-start = ((), (), s32[]{:S(2)}) async-start(), calls=%async_computation.1 | async-start | bytes 1572864 | tf_op jit(solution)/shard_map/all_gather | solution.py:66
  175.7 0.9 copy-start.2
  177.4 60.9 %all-gather.10.cloned.1.call-start = ((), (), s32[]{:S(2)}) async-start(), calls=%async_computation.2 | async-start | bytes 2359296 | tf_op jit(solution)/shard_map/all_gather | solution.py:77
  199.9 3.0 %copy-start.3 = (bf16[2048,256]{1,0:T(8,128)(2,1)S(1)}, bf16[2048,256]{1,0:T(8,128)(2,1)}, u32[]{:S(2)}) copy-start(bf16[2048,256]{1,0:T(8,128)(2,1)} %all-gather.8.cloned.1.call-done) | copy-start | bytes 3145732
  242.0 30.2 %collective-permute-start = (bf16[1,1024,640]{2,1,0:T(8,128)(2,1)S(1)}, bf16[1,1024,640]{2,1,0:T(8,128)(2,1)S(1)}, u32[]{:S(2)}, u32[]{:S(2)}) collective-permute-start(bf16[1,1024,640]{2,1,0:T(8,128)(2,1)S(1)} %fusion.9), channel_id=1, source_target_pairs={{16,0},{0,16},{17,1},{1,17},{18,2},{2,18},{19,3},{3,19},{20,4},{4,... | collective-permute-start | bytes 3932168 | tf_op jit(solution)/shard_map/ppermute | solution.py:14
Sparse Core Ops, SparseCore 0:
  8.9 55.8 all-gather.11
  66.4 99.7 all-gather.5
  177.6 19.2 all-gather.7
  207.0 31.2 all-gather.9
where the time goes:
time: 281 us; the launch traced here: 280 us
  waiting for transfers between devices  208 us (74%)
  matrix products  20.1 us (7%)
  local copies, waits for them, and re-layouts  17.7 us (6%)
  blocking collectives  14.6 us (5%)
  between operations  13.3 us (5%)
  other arithmetic  5.13 us (2%)
    all_gather x1, waiting for transfers between devices, shards(): normed = lax.all_gather(normed_part, 'dp', axis=1, tiled=True)  101 us
    all_gather x1, waiting for transfers between devices, shards(): lax.all_gather(weight_half, 'seq', axis=0, tiled=True)  40.3 us
    all_gather x1, waiting for transfers between devices, shards(): lax.all_gather(attended, 'dp', axis=1, tiled=True)  31.4 us
    ppermute x1, waiting for transfers between devices, shifted(): return lax.ppermute(block, axis, route)  29.2 us
    psum x1, blocking collectives, shards(): total_squares = lax.psum(local_squares, 'dp')  14.6 us
    broadcast_in_dim x2, local copies, waits for them, and re-layouts, sparse_attention(): weights = jnp.where(live, jnp.exp(scores - highest), 0.0)  14.2 us
    dot_general x1, matrix products, shards(): jnp.dot(normed, lax.all_gather(weight_half, 'seq', axis=0, tiled=True), p...  9.44 us
  transfers between devices with their start and end apart: 5, of which 5 were waited for; matrix products, arithmetic and copies ran while one was open for 6% of the time, Pallas kernels for 0%

commit v1 on v0

--- a/solution.py
+++ b/solution.py
@@ -1,8 +1,11 @@
+import functools
 import math
 
 import jax
 import jax.numpy as jnp
 from jax import lax
+from jax.experimental import pallas as pl
+from jax.experimental.pallas import tpu as pltpu
 from jax.sharding import PartitionSpec as P
 
 BLOCK = 64
@@ -82,6 +85,419 @@
     return shifted(result[None], "section", 1)
 
 
+CHUNKS = 4
+
+
+def relay_kernel(
+    nz,
+    x_ref,
+    gain_ref,
+    w_ref,
+    ow_ref,
+    rand_ref,
+    glob_ref,
+    out_ref,
+    x_all,
+    w_all,
+    g_all,
+    acc,
+    squares,
+    q_s,
+    kv,
+    bias,
+    m_s,
+    l_s,
+    o_s,
+    att_own,
+    att_all,
+    x_next,
+    ow_next,
+    xs,
+    xr,
+    ws,
+    wr,
+    gs,
+    gr,
+    ks,
+    kr,
+    ts,
+    tr,
+    as_,
+    ar,
+    ns,
+    nr,
+    local,
+):
+    sec, p, y = lax.axis_index("section"), lax.axis_index("dp"), lax.axis_index("seq")
+    dp = 2 * nz
+    z, core = p // 2, p % 2
+    sib = p + 1 - 2 * core
+    tokens, feats = x_ref.shape
+    width = feats * dp
+    rows = tokens // CHUNKS
+    head = q_s.shape[1]
+    half = dp // 2
+    scale = math.log2(math.e) / math.sqrt(head)
+
+    barrier = pltpu.get_barrier_semaphore()
+    for step in range(1, dp):
+        pl.semaphore_signal(
+            barrier, inc=1, device_id={"dp": lax.rem(p + step, dp)},
+            device_id_type=pl.DeviceIdType.MESH,
+        )
+    for name, at in (("seq", 1 - y), ("section", 1 - sec)):
+        pl.semaphore_signal(
+            barrier, inc=1, device_id={name: at}, device_id_type=pl.DeviceIdType.MESH
+        )
+
+    def remote(src, dst, send, recv, where):
+        return pltpu.make_async_remote_copy(
+            src_ref=src, dst_ref=dst, send_sem=send, recv_sem=recv,
+            device_id=where, device_id_type=pl.DeviceIdType.MESH,
+        )
+
+    def part(k):
+        return pl.ds(k * rows, rows)
+
+    def chunk(k):
+        return pl.ds(pl.multiple_of(k * rows, rows), rows)
+
+    own_x = pltpu.make_async_copy(x_ref, x_all.at[p], local.at[0])
+    own_w = pltpu.make_async_copy(
+        w_ref, w_all.at[pl.ds(pl.multiple_of(y * half * feats, feats), half * feats), :], local.at[1]
+    )
+    own_x.start()
+    own_w.start()
+    g_all[p] = jnp.broadcast_to(gain_ref[...].astype(jnp.float32), (8, feats))
+
+    pl.semaphore_wait(barrier, dp + 1)
+
+    def hop(buf, send, recv, way, b, k, src=None):
+        at = buf.at[b, part(k), :]
+        to = (p - 2, p + 2, sib)[way]
+        return remote(at if src is None else src, at, send.at[way, b, k], recv.at[b, k], {"dp": to})
+
+    def spread(buf, send, recv, b, k, ways, act, src=None):
+        if 0 in ways:
+            @pl.when(z > 0)
+            def _():
+                act(hop(buf, send, recv, 0, b, k, src))
+        if 1 in ways:
+            @pl.when(z < nz - 1)
+            def _():
+                act(hop(buf, send, recv, 1, b, k, src))
+        act(hop(buf, send, recv, 2, b, k, src))
+
+    start = lambda copy: copy.start()
+    sent = lambda copy: copy.wait_send()
+
+    def chain(buf, send, recv, d, k):
+        @pl.when(z + d < nz)
+        def _():
+            b = p + 2 * d
+            hop(buf, send, recv, 2, b, k).wait_recv()
+            spread(buf, send, recv, b, k, (0,), start)
+
+        @pl.when(z - d >= 0)
+        def _():
+            b = p - 2 * d
+            hop(buf, send, recv, 2, b, k).wait_recv()
+            spread(buf, send, recv, b, k, (1,), start)
+
+    def drain(buf, send, recv, k, src=None):
+        spread(buf, send, recv, p, k, (0, 1), sent, src)
+        for d in range(1, nz):
+            @pl.when(z + d < nz)
+            def _():
+                spread(buf, send, recv, p + 2 * d, k, (0,), sent)
+
+            @pl.when(z - d >= 0)
+            def _():
+                spread(buf, send, recv, p - 2 * d, k, (1,), sent)
+
+    for k in range(CHUNKS):
+        spread(x_all, xs, xr, p, k, (0, 1), start, x_ref.at[part(k), :])
+
+    def gain_copy(to, src):
+        return remote(g_all.at[src], g_all.at[src], gs.at[to], gr.at[src], {"dp": to})
+
+    for step in range(1, dp):
+        gain_copy(lax.rem(p + step, dp), p).start()
+
+    flip = jnp.where(y == 0, jnp.where(z >= 1, 1, 0), jnp.where(z >= nz - 1, 1, 0)) * (half // 2)
+
+    def w_copy(j, whose):
+        block = lax.rem(j + flip, half) if whose is None else whose
+        mine = pl.ds(pl.multiple_of(block * feats, feats), feats)
+        there = pl.ds(pl.multiple_of((y * half + block) * feats, feats), feats)
+        return remote(w_ref.at[mine, :], w_all.at[there, :], ws.at[block], wr.at[block], {"seq": 1 - y})
+
+    for j in range(half):
+        w_copy(j, None).start()
+
+    next_x = remote(x_ref, x_next, ns.at[0], nr.at[0], {"section": 1 - sec})
+    next_w = remote(ow_ref, ow_next, ns.at[1], nr.at[1], {"section": 1 - sec})
+    next_x.start()
+    next_w.start()
+
+    acc[...] = jnp.zeros_like(acc)
+    squares[...] = jnp.zeros_like(squares)
+
+    blocks = tokens // BLOCK
+    for h in range(2):
+        key_at = y if h == 0 else 1 - y
+        lane = lax.broadcasted_iota(jnp.int32, (blocks, tokens), 1)
+        key_id = lane // BLOCK + key_at * blocks
+        query_id = lax.broadcasted_iota(jnp.int32, (blocks, tokens), 0) + y * blocks
+        allowed = jnp.abs(query_id - key_id) <= 1
+        for g in range(glob_ref.shape[1]):
+            number = glob_ref[:, g : g + 1]
+            allowed = allowed | (key_id == number) | (query_id == number)
+        for r in range(rand_ref.shape[1]):
+            allowed = allowed | (key_id == rand_ref[:, r : r + 1])
+        bias[h] = jnp.where(allowed, 0.0, -jnp.inf)
+
+    def project(b, k):
+        xb = x_all[b, chunk(k), :].astype(jnp.float32)
+        sq = xb * xb
+        folded = sq[:, :128]
+        for c in range(1, feats // 128):
+            folded = folded + sq[:, c * 128 : (c + 1) * 128]
+        squares[chunk(k), :] += folded
+        xg = (xb * g_all[b, 0:1, :]).astype(jnp.bfloat16)
+        wb = w_all[pl.ds(pl.multiple_of(b * feats, feats), feats), :]
+        acc[chunk(k), :] += jnp.dot(xg, wb, preferred_element_type=jnp.float32)
+
+    def ready(b):
+        @pl.when(b != p)
+        def _():
+            gain_copy(sib, b).wait_recv()
+
+        @pl.when(b // half != y)
+        def _():
+            w_copy(0, b % half).wait_recv()
+
+    def each(d, fn):
+        if d == 0:
+            fn(p, False)
+            fn(sib, True)
+            return
+
+        @pl.when(z + d < nz)
+        def _():
+            fn(p + 2 * d, False)
+            fn(sib + 2 * d, True)
+
+        @pl.when(z - d >= 0)
+        def _():
+            fn(p - 2 * d, False)
+            fn(sib - 2 * d, True)
+
+    def from_sib(b, k):
+        hop(x_all, xs, xr, 2, b, k).wait_recv()
+
+    def whole_step(d):
+        def one(b, other):
+            ready(b)
+            if other:
+                for k in range(CHUNKS):
+                    from_sib(b, k)
+
+            def body(k, _):
+                project(b, k)
+                return 0
+
+            lax.fori_loop(0, CHUNKS, body, 0)
+
+        each(d, one)
+
+    def kv_copy(k):
+        return remote(kv.at[0, part(k), :], kv.at[1, part(k), :], ks.at[k], kr.at[k], {"seq": 1 - y})
+
+    def last_step(k):
+        def one(b, other):
+            if k == 0:
+                ready(b)
+            if other:
+                from_sib(b, k)
+            project(b, k)
+
+        if nz > 1:
+            each(nz - 1, one)
+        total = jnp.sum(squares[part(k), :], axis=1, keepdims=True)
+        joined = acc[part(k), :] * lax.rsqrt(total / width + 1e-05)
+        q_s[part(k), :] = joined[:, :head].astype(jnp.bfloat16)
+        kv[0, part(k), :] = joined[:, head:].astype(jnp.bfloat16)
+        kv_copy(k).start()
+
+    own_x.wait()
+    own_w.wait()
+    for d in range(1, nz):
+        for k in range(CHUNKS):
+            chain(x_all, xs, xr, d, k)
+            if d == nz - 2 and k == 1:
+                for e in range(0, nz - 3):
+                    whole_step(e)
+            if d == nz - 2 and k == 2:
+                whole_step(nz - 3)
+            if d == nz - 1 and k == 0:
+                whole_step(nz - 2)
+            if d == nz - 1 and k > 0:
+                last_step(k - 1)
+    last_step(CHUNKS - 1)
+
+    per = blocks // CHUNKS
+
+    def scores_of(k, h):
+        s = lax.dot_general(
+            q_s[part(k), :], kv[h, :, :head], (((1,), (1,)), ((), ())),
+            preferred_element_type=jnp.float32,
+        )
+        s = (s * scale).reshape(per, BLOCK, tokens)
+        s = s + bias[h, k * per : (k + 1) * per, :][:, None, :]
+        return s.reshape(rows, tokens)
+
+    def own_keys(k):
+        s = scores_of(k, 0)
+        m = jnp.max(s, axis=1, keepdims=True)
+        e = jnp.exp2(s - m)
+        m_s[part(k), :] = m
+        l_s[part(k), :] = jnp.sum(e, axis=1, keepdims=True)
+        o_s[part(k), :] = jnp.dot(
+            e.astype(jnp.bfloat16), kv[0, :, head:], preferred_element_type=jnp.float32
+        )
+
+    def att_copy(k):
+        return remote(
+            att_own.at[part(k), :], att_all.at[p, part(k), :], ts.at[k], ar.at[p, k], {"section": 1 - sec}
+        )
+
+    def other_keys(k):
+        s = scores_of(k, 1)
+        before = m_s[part(k), :]
+        m = jnp.maximum(before, jnp.max(s, axis=1, keepdims=True))
+        e = jnp.exp2(s - m)
+        shrink = jnp.exp2(before - m)
+        total = l_s[part(k), :] * shrink + jnp.sum(e, axis=1, keepdims=True)
+        o = o_s[part(k), :] * shrink + jnp.dot(
+            e.astype(jnp.bfloat16), kv[1, :, head:], preferred_element_type=jnp.float32
+        )
+        att_own[part(k), :] = (o / total).astype(jnp.bfloat16)
+        att_copy(k).start()
+
+    for k in range(CHUNKS):
+        own_keys(k)
+    for k in range(CHUNKS):
+        kv_copy(k).wait_recv()
+    next_x.wait_recv()
+    next_w.wait_recv()
+
+    def att_step(d, k):
+        if d == 0:
+            att_copy(k).wait_recv()
+            spread(att_all, as_, ar, p, k, (0, 1), start)
+        else:
+            chain(att_all, as_, ar, d, k)
+
+    def finish(k):
+        hop(att_all, as_, ar, 2, sib, k).wait_recv()
+        for d in range(1, nz):
+            @pl.when(z + d < nz)
+            def _():
+                hop(att_all, as_, ar, 2, sib + 2 * d, k).wait_recv()
+
+            @pl.when(z - d >= 0)
+            def _():
+                hop(att_all, as_, ar, 2, sib - 2 * d, k).wait_recv()
+        heads = jnp.concatenate([att_all[b, part(k), :] for b in range(dp)], axis=1)
+        added = jnp.dot(heads, ow_next[...], preferred_element_type=jnp.float32)
+        out_ref[part(k), :] = (x_next[part(k), :].astype(jnp.float32) + added).astype(jnp.bfloat16)
+
+    for i in range(CHUNKS + nz + 1):
+        if i < CHUNKS:
+            other_keys(i)
+        for d in range(nz):
+            if 0 <= i - 1 - d < CHUNKS:
+                att_step(d, i - 1 - d)
+        if 0 <= i - nz - 1 < CHUNKS:
+            finish(i - nz - 1)
+
+    for k in range(CHUNKS):
+        drain(x_all, xs, xr, k)
+        drain(att_all, as_, ar, k)
+        kv_copy(k).wait_send()
+        att_copy(k).wait_send()
+    for step in range(1, dp):
+        gain_copy(lax.rem(p + step, dp), p).wait_send()
+    for j in range(half):
+        w_copy(j, None).wait_send()
+    next_x.wait_send()
+    next_w.wait_send()
+
+
+def relay(dp, x, gain, w, ow, rand, glob):
+    nz = dp // 2
+    tokens, feats = x.shape
+    columns = w.shape[1]
+    head = columns // 3
+    vmem = pl.BlockSpec(memory_space=pltpu.VMEM)
+    anywhere = pl.BlockSpec(memory_space=pl.ANY)
+    bf16, f32, dma = jnp.bfloat16, jnp.float32, pltpu.SemaphoreType.DMA
+    return pl.pallas_call(
+        functools.partial(relay_kernel, nz),
+        out_shape=jax.ShapeDtypeStruct((tokens, feats), bf16),
+        in_specs=[anywhere, vmem, anywhere, anywhere, vmem, vmem],
+        out_specs=vmem,
+        scratch_shapes=[
+            pltpu.VMEM((dp, tokens, feats), bf16),
+            pltpu.VMEM((dp * feats, columns), bf16),
+            pltpu.VMEM((dp, 8, feats), f32),
+            pltpu.VMEM((tokens, columns), f32),
+            pltpu.VMEM((tokens, 128), f32),
+            pltpu.VMEM((tokens, head), bf16),
+            pltpu.VMEM((2, tokens, 2 * head), bf16),
+            pltpu.VMEM((2, tokens // BLOCK, tokens), f32),
+            pltpu.VMEM((tokens, 1), f32),
+            pltpu.VMEM((tokens, 1), f32),
+            pltpu.VMEM((tokens, head), f32),
+            pltpu.VMEM((tokens, head), bf16),
+            pltpu.VMEM((dp, tokens, head), bf16),
+            pltpu.VMEM((tokens, feats), bf16),
+            pltpu.VMEM(ow.shape, bf16),
+            dma((3, dp, CHUNKS)),
+            dma((dp, CHUNKS)),
+            dma((dp // 2,)),
+            dma((dp // 2,)),
+            dma((dp,)),
+            dma((dp,)),
+            dma((CHUNKS,)),
+            dma((CHUNKS,)),
+            dma((CHUNKS,)),
+            dma((CHUNKS,)),
+            dma((3, dp, CHUNKS)),
+            dma((dp, CHUNKS)),
+            dma((2,)),
+            dma((2,)),
+            dma((2,)),
+        ],
+        compiler_params=pltpu.CompilerParams(
+            collective_id=0, has_side_effects=True, vmem_limit_bytes=56 * 1024 * 1024
+        ),
+        name="relay_layer",
+    )(x, gain, w, ow, rand, glob)
+
+
+def tiles(mesh, tokens, feats, columns):
+    return (
+        mesh.shape["section"] == 2
+        and mesh.shape["seq"] == 2
+        and mesh.shape["dp"] == 8
+        and feats % 128 == 0
+        and columns % 384 == 0
+        and tokens % (CHUNKS * BLOCK) == 0
+    )
+
+
 def solution(mesh):
     placed = (
         P("section", "seq", "dp"),
@@ -91,6 +507,18 @@
         P("section", "seq", None),
         P("section", None),
     )
+
+    def layer(section_input, norm_gain, qkv_weight, out_weight, random_blocks, global_blocks):
+        args = (section_input, norm_gain, qkv_weight, out_weight, random_blocks, global_blocks)
+        _, tokens, feats = section_input.shape
+        if not tiles(mesh, tokens, feats, qkv_weight.shape[2]):
+            return shards(*args)
+        out = relay(
+            mesh.shape["dp"], section_input[0], norm_gain, qkv_weight[0], out_weight[0],
+            random_blocks[0], global_blocks,
+        )
+        return out[None]
+
     return jax.shard_map(
-        shards, mesh=mesh, in_specs=placed, out_specs=P("section", "seq", "dp"), check_vma=False
-    )
+        layer, mesh=mesh, in_specs=placed, out_specs=P("section", "seq", "dp"), check_vma=False
+    )

time: 281 us -> 134 us (0.48)
  waiting for transfers between devices: 208 us -> 0 us
  Pallas kernels: 0 us -> 130 us
  matrix products: 20.1 us -> 0 us
  blocking collectives: 14.6 us -> 0 us
  local copies, waits for them, and re-layouts: 17.7 us -> 3.84 us
  between operations: 13.3 us -> 0.01 us
  other arithmetic: 5.13 us -> 0 us
    all_gather x4 -> x0, waiting for transfers between devices: 178 us -> none  [the longest x1 101 us: shards(): normed = lax.all_gather(normed_part, 'dp', axis=1, tiled=True)]
    pallas_call x0 -> x1, Pallas kernels: none -> 130 us  [relay(): pl.pallas_call(functools.partial(relay_kernel, nz), out_shape=jax.ShapeDt...]
    ppermute x1 -> x0, waiting for transfers between devices: 29.2 us -> none  [shifted(): return lax.ppermute(block, axis, route)]
    dot_general x4 -> x0, matrix products: 20.1 us -> none  [the longest x1 9.44 us: shards(): jnp.dot(normed, lax.all_gather(weight_half, 'seq', axis=0, tiled=True), p...]
    psum x1 -> x0, blocking collectives: 14.6 us -> none  [shards(): total_squares = lax.psum(local_squares, 'dp')]
    broadcast_in_dim x2 -> x0, local copies, waits for them, and re-layouts: 14.2 us -> none  [sparse_attention(): weights = jnp.where(live, jnp.exp(scores - highest), 0.0)]
    reduce_sum x2 -> x0, other arithmetic: 3.34 us -> none  [the longest x1 3.01 us: sparse_attention(): totals = jnp.sum(weights, axis=(2, 3), keepdims=True)]
  transfers between devices with their start and end apart: 5 -> 0, of which waited for: 5 -> 0; matrix products, arithmetic and copies ran while one was open for 6% -> 0% of each run, Pallas kernels for 0% -> 0%
where the time goes in v1:
time: 134 us
  Pallas kernels  130 us (97%)
  local copies, waits for them, and re-layouts  3.84 us (3%)
    pallas_call x1, Pallas kernels, relay(): pl.pallas_call(functools.partial(relay_kernel, nz), out_shape=jax.ShapeDt...  130 us

profile of v1, /device:TPU:1, one launch (start us, length us, event | category | flops | bytes accessed | tf_op | source)
XLA Modules:
  0.0 133.6 jit_solution(16732133048547055863)
XLA Ops:
  0.0 1.4 %copy.8 = s32[1,16,3]{2,1,0:T(8,128)} copy(s32[1,16,3]{1,0,2:T(1,128)} %param.10) | data formatting | bytes 384 | tf_op jit(solution)/shard_map/squeeze | solution.py:518
  1.4 129.8 %relay_layer.1 = bf16[1024,640]{1,0:T(8,128)(2,1)} custom-call(bf16[1024,640]{1,0:T(8,128)(2,1)} %bitcast.7, bf16[1,640]{1,0:T(2,128)(2,1)} %gain_ref.1, bf16[2560,384]{1,0:T(8,128)(2,1)} %bitcast.6, bf16[1024,640]{1,0:T(8,128)(2,1)} %bitcast.8, s32[16,3]{1,0:T(8,128)} %bitcast.9, s32[1,2]{1,0:T(1,128)} %glob_ref.1), custom_call_target="tpu_custom_call" | custom-call | tf_op jit(solution)/shard_map/relay_layer/pallas_call | solution.py:446
  131.1 2.5 %copy.10 = bf16[1,1024,640]{2,1,0:T(8,128)(2,1)} copy(bf16[1,1024,640]{2,1,0:T(8,128)(2,1)} %bitcast.5) | data formatting | bytes 2621440

commit v2 on v1

--- a/solution.py
+++ b/solution.py
@@ -101,7 +101,6 @@
     w_all,
     g_all,
     acc,
-    squares,
     q_s,
     kv,
     bias,
@@ -112,6 +111,12 @@
     att_all,
     x_next,
     ow_next,
+    w_far,
+    part_out,
+    part_in,
+    ss_out,
+    ss_in,
+    total_s,
     xs,
     xr,
     ws,
@@ -126,6 +131,10 @@
     ar,
     ns,
     nr,
+    fs,
+    fr,
+    ps,
+    pr,
     local,
 ):
     sec, p, y = lax.axis_index("section"), lax.axis_index("dp"), lax.axis_index("seq")
@@ -215,25 +224,84 @@
             def _():
                 spread(buf, send, recv, p - 2 * d, k, (1,), sent)
 
-    for k in range(CHUNKS):
-        spread(x_all, xs, xr, p, k, (0, 1), start, x_ref.at[part(k), :])
+    near = z // (nz // 2)
+    far = 1 - near
+    inward = 2 - 4 * near
+    is_end = (z == 0) | (z == nz - 1)
+    is_helper = jnp.logical_not(is_end)
+    in_far, in_near = y == far, y != far
+    mate, end, far_end = p + inward, p - inward, p + 2 * inward
+
+    def other(b):
+        return b + 1 - 2 * core
+
+    def xhop(way, b, k, own=False):
+        at = x_all.at[b, part(k), :]
+        to = (p + inward, p - inward, sib)[way]
+        src = x_ref.at[part(k), :] if own else at
+        return remote(src, at, xs.at[way, b, k], xr.at[b, k], {"dp": to})
+
+    def arrived(b, k, *ways):
+        xhop(2, b, k).wait_recv()
+        for way in ways:
+            xhop(way, b, k).start()
+
+    def rows_of(j):
+        return pl.ds(pl.multiple_of(j * feats, feats), feats)
+
+    def w_copy(j):
+        return remote(
+            w_ref.at[rows_of(j), :], w_all.at[rows_of(y * half + j), :], ws.at[j], wr.at[j],
+            {"seq": 1 - y},
+        )
+
+    def far_copy(j, src, where):
+        return remote(src, w_far.at[rows_of(j), :], fs.at[j], fr.at[j], where)
+
+    def far_from_end(j):
+        return far_copy(j, w_ref.at[rows_of(j), :], {"dp": mate})
+
+    def far_passed(j):
+        return far_copy(j, w_all.at[rows_of(far * half + j), :], {"dp": mate})
+
+    def far_shared(j):
+        return far_copy(j, w_far.at[rows_of(j), :], {"seq": 1 - y})
 
     def gain_copy(to, src):
         return remote(g_all.at[src], g_all.at[src], gs.at[to], gr.at[src], {"dp": to})
 
+    quarter = half // 2
+    first_w = (1 - y) * quarter
+    rest_w = y * quarter
+
+    @pl.when(is_helper)
+    def _():
+        for k in range(CHUNKS):
+            for way in (0, 1, 2):
+                xhop(way, p, k, True).start()
+        for j in range(quarter):
+            w_copy(first_w + j).start()
+
+    @pl.when(is_end & in_far)
+    def _():
+        for j in range(quarter):
+            far_from_end(j).start()
+            w_copy(quarter + j).start()
+        for k in range(CHUNKS):
+            xhop(0, p, k, True).start()
+            xhop(2, p, k, True).start()
+
+    @pl.when(is_end & in_near)
+    def _():
+        for k in range(CHUNKS // 2):
+            xhop(0, p, k, True).start()
+        for k in range(CHUNKS):
+            xhop(2, p, k, True).start()
+        for j in range(half):
+            w_copy(j).start()
+
     for step in range(1, dp):
         gain_copy(lax.rem(p + step, dp), p).start()
-
-    flip = jnp.where(y == 0, jnp.where(z >= 1, 1, 0), jnp.where(z >= nz - 1, 1, 0)) * (half // 2)
-
-    def w_copy(j, whose):
-        block = lax.rem(j + flip, half) if whose is None else whose
-        mine = pl.ds(pl.multiple_of(block * feats, feats), feats)
-        there = pl.ds(pl.multiple_of((y * half + block) * feats, feats), feats)
-        return remote(w_ref.at[mine, :], w_all.at[there, :], ws.at[block], wr.at[block], {"seq": 1 - y})
-
-    for j in range(half):
-        w_copy(j, None).start()
 
     next_x = remote(x_ref, x_next, ns.at[0], nr.at[0], {"section": 1 - sec})
     next_w = remote(ow_ref, ow_next, ns.at[1], nr.at[1], {"section": 1 - sec})
@@ -241,7 +309,6 @@
     next_w.start()
 
     acc[...] = jnp.zeros_like(acc)
-    squares[...] = jnp.zeros_like(squares)
 
     blocks = tokens // BLOCK
     for h in range(2):
@@ -257,94 +324,190 @@
             allowed = allowed | (key_id == rand_ref[:, r : r + 1])
         bias[h] = jnp.where(allowed, 0.0, -jnp.inf)
 
+    def scaled(b, k):
+        return (x_all[b, chunk(k), :].astype(jnp.float32) * g_all[b, 0:1, :]).astype(jnp.bfloat16)
+
     def project(b, k):
-        xb = x_all[b, chunk(k), :].astype(jnp.float32)
-        sq = xb * xb
-        folded = sq[:, :128]
-        for c in range(1, feats // 128):
-            folded = folded + sq[:, c * 128 : (c + 1) * 128]
-        squares[chunk(k), :] += folded
-        xg = (xb * g_all[b, 0:1, :]).astype(jnp.bfloat16)
-        wb = w_all[pl.ds(pl.multiple_of(b * feats, feats), feats), :]
-        acc[chunk(k), :] += jnp.dot(xg, wb, preferred_element_type=jnp.float32)
-
-    def ready(b):
-        @pl.when(b != p)
-        def _():
-            gain_copy(sib, b).wait_recv()
-
-        @pl.when(b // half != y)
-        def _():
-            w_copy(0, b % half).wait_recv()
-
-    def each(d, fn):
-        if d == 0:
-            fn(p, False)
-            fn(sib, True)
-            return
-
-        @pl.when(z + d < nz)
-        def _():
-            fn(p + 2 * d, False)
-            fn(sib + 2 * d, True)
-
-        @pl.when(z - d >= 0)
-        def _():
-            fn(p - 2 * d, False)
-            fn(sib - 2 * d, True)
+        acc[chunk(k), :] += jnp.dot(
+            scaled(b, k), w_all[rows_of(b), :], preferred_element_type=jnp.float32
+        )
+
+    def project_whole(b):
+        def body(k, _):
+            project(b, k)
+            return 0
+
+        lax.fori_loop(0, CHUNKS, body, 0)
 
     def from_sib(b, k):
-        hop(x_all, xs, xr, 2, b, k).wait_recv()
-
-    def whole_step(d):
-        def one(b, other):
-            ready(b)
-            if other:
-                for k in range(CHUNKS):
-                    from_sib(b, k)
-
-            def body(k, _):
-                project(b, k)
-                return 0
-
-            lax.fori_loop(0, CHUNKS, body, 0)
-
-        each(d, one)
+        xhop(2, b, k).wait_recv()
 
     def kv_copy(k):
         return remote(kv.at[0, part(k), :], kv.at[1, part(k), :], ks.at[k], kr.at[k], {"seq": 1 - y})
 
-    def last_step(k):
-        def one(b, other):
-            if k == 0:
-                ready(b)
-            if other:
-                from_sib(b, k)
-            project(b, k)
-
-        if nz > 1:
-            each(nz - 1, one)
-        total = jnp.sum(squares[part(k), :], axis=1, keepdims=True)
-        joined = acc[part(k), :] * lax.rsqrt(total / width + 1e-05)
+    def finish_joined(k, joined, total):
+        joined = joined * lax.rsqrt(total / width + 1e-05)
         q_s[part(k), :] = joined[:, :head].astype(jnp.bfloat16)
         kv[0, part(k), :] = joined[:, head:].astype(jnp.bfloat16)
         kv_copy(k).start()
 
-    own_x.wait()
-    own_w.wait()
-    for d in range(1, nz):
-        for k in range(CHUNKS):
-            chain(x_all, xs, xr, d, k)
-            if d == nz - 2 and k == 1:
-                for e in range(0, nz - 3):
-                    whole_step(e)
-            if d == nz - 2 and k == 2:
-                whole_step(nz - 3)
-            if d == nz - 1 and k == 0:
-                whole_step(nz - 2)
-            if d == nz - 1 and k > 0:
-                last_step(k - 1)
-    last_step(CHUNKS - 1)
+    def part_copies(k):
+        return (
+            remote(part_out.at[part(k), :], part_in.at[part(k), :], ps.at[0, k], pr.at[0, k], {"dp": end}),
+            remote(ss_out.at[k], ss_in.at[k], ps.at[1, k], pr.at[1, k], {"dp": end}),
+        )
+
+    def diagonal():
+        return lax.broadcasted_iota(jnp.int32, (rows, rows), 0) == lax.broadcasted_iota(
+            jnp.int32, (rows, rows), 1
+        )
+
+    def help_end(k):
+        if k == 0:
+            @pl.when(in_far)
+            def _():
+                for j in range(quarter, half):
+                    far_shared(j).wait_recv()
+
+            @pl.when(in_near)
+            def _():
+                for j in range(quarter):
+                    far_shared(j).wait_recv()
+
+        from_sib(other(end), k)
+        from_sib(other(far_end), k)
+        part_sum = jnp.zeros((rows, acc.shape[1]), jnp.float32)
+        for j in range(half):
+            part_sum += jnp.dot(
+                scaled(far * half + j, k), w_far[pl.ds(j * feats, feats), :],
+                preferred_element_type=jnp.float32,
+            )
+        part_out[part(k), :] = part_sum.astype(jnp.bfloat16)
+        folded = jnp.zeros((rows, 128), jnp.float32)
+        for b in range(dp):
+            for c in range(feats // 128):
+                xb = x_all[b, part(k), c * 128 : (c + 1) * 128].astype(jnp.float32)
+                folded += xb * xb
+        total = jnp.sum(folded, axis=1, keepdims=True)
+        total_s[part(k), :] = total
+        across = jnp.sum(
+            jnp.where(diagonal(), jnp.broadcast_to(total, (rows, rows)), 0.0), axis=0, keepdims=True
+        )
+        ss_out[k] = jnp.broadcast_to(across, (8, rows))
+        for copy in part_copies(k):
+            copy.start()
+
+    def all_gains():
+        for step in range(1, dp):
+            gain_copy(sib, lax.rem(p + step, dp)).wait_recv()
+
+    @pl.when(is_end)
+    def _():
+        @pl.when(in_near)
+        def _():
+            for j in range(quarter):
+                w_copy(quarter + j).wait_recv()
+                far_passed(quarter + j).start()
+                for k in range(CHUNKS // 2 + j, CHUNKS, quarter):
+                    xhop(0, p, k, True).start()
+
+        for k in range(CHUNKS):
+            arrived(mate, k, 2)
+        own_x.wait()
+        own_w.wait()
+        all_gains()
+
+        @pl.when(in_far)
+        def _():
+            for j in range(half):
+                w_copy(j).wait_recv()
+
+        for k in range(CHUNKS):
+            from_sib(sib, k)
+            from_sib(other(mate), k)
+        for b in (p, sib, mate, other(mate)):
+            project_whole(b)
+        for k in range(CHUNKS):
+            for copy in part_copies(k):
+                copy.wait_recv()
+            total = jnp.sum(
+                jnp.where(diagonal(), jnp.broadcast_to(ss_in[k, 0:1, :], (rows, rows)), 0.0),
+                axis=1, keepdims=True,
+            )
+            finish_joined(k, acc[part(k), :] + part_in[part(k), :].astype(jnp.float32), total)
+
+    @pl.when(is_helper)
+    def _():
+        def share(j):
+            far_shared(j).wait_recv()
+            far_shared(j).start()
+
+        def rest_of_w():
+            for j in range(quarter):
+                w_copy(rest_w + j).start()
+
+        @pl.when(in_far)
+        def _():
+            arrived(mate, 0, 2)
+            share(0)
+            arrived(mate, 1, 2)
+            arrived(mate, 2, 2)
+            share(1)
+            rest_of_w()
+            arrived(mate, 3, 2)
+            arrived(end, 0, 0, 2)
+            arrived(end, 1, 0, 2)
+
+        @pl.when(in_near)
+        def _():
+            arrived(mate, 0, 2)
+            arrived(end, 0, 0, 2)
+            arrived(mate, 1, 2)
+            arrived(end, 1, 0, 2)
+            arrived(mate, 2, 2)
+            share(2)
+            arrived(mate, 3, 2)
+            rest_of_w()
+            arrived(end, 2, 0, 2)
+            share(3)
+
+        own_x.wait()
+        own_w.wait()
+        all_gains()
+        for j in range(quarter):
+            w_copy(rest_w + j).wait_recv()
+        for k in range(CHUNKS):
+            from_sib(sib, k)
+            from_sib(other(mate), k)
+        for b in (p, sib, mate, other(mate)):
+            project_whole(b)
+
+        held = jnp.where(near == y, end, far_end)
+        missing = jnp.where(near == y, far_end, end)
+
+        def help_and_project(k):
+            help_end(k)
+            project(held, k)
+            project(other(held), k)
+
+        for k in range(CHUNKS):
+            if k == 2:
+                @pl.when(in_far)
+                def _():
+                    arrived(end, 2, 0, 2)
+
+            if k == 3:
+                arrived(end, 3, 0, 2)
+            arrived(far_end, k, 2)
+            if k > 0:
+                help_and_project(k - 1)
+        help_and_project(CHUNKS - 1)
+        for j in range(quarter):
+            w_copy(first_w + j).wait_recv()
+        for k in range(CHUNKS):
+            project(missing, k)
+            project(other(missing), k)
+            finish_joined(k, acc[part(k), :], total_s[part(k), :])
 
     per = blocks // CHUNKS
 
@@ -423,14 +586,39 @@
             finish(i - nz - 1)
 
     for k in range(CHUNKS):
-        drain(x_all, xs, xr, k)
         drain(att_all, as_, ar, k)
         kv_copy(k).wait_send()
         att_copy(k).wait_send()
+        xhop(2, p, k, True).wait_send()
+        xhop(0, p, k, True).wait_send()
+        xhop(2, mate, k).wait_send()
+
+        @pl.when(is_helper)
+        def _():
+            xhop(1, p, k, True).wait_send()
+            xhop(0, end, k).wait_send()
+            xhop(2, end, k).wait_send()
+            xhop(2, far_end, k).wait_send()
+            for copy in part_copies(k):
+                copy.wait_send()
+
     for step in range(1, dp):
         gain_copy(lax.rem(p + step, dp), p).wait_send()
-    for j in range(half):
-        w_copy(j, None).wait_send()
+    for j in range(quarter):
+        w_copy(quarter + j).wait_send()
+
+        @pl.when(jnp.logical_not(is_end & in_far))
+        def _():
+            w_copy(j).wait_send()
+
+        @pl.when(in_far)
+        def _():
+            far_shared(j).wait_send()
+
+        @pl.when(in_near)
+        def _():
+            far_shared(quarter + j).wait_send()
+
     next_x.wait_send()
     next_w.wait_send()
 
@@ -453,7 +641,6 @@
             pltpu.VMEM((dp * feats, columns), bf16),
             pltpu.VMEM((dp, 8, feats), f32),
             pltpu.VMEM((tokens, columns), f32),
-            pltpu.VMEM((tokens, 128), f32),
             pltpu.VMEM((tokens, head), bf16),
             pltpu.VMEM((2, tokens, 2 * head), bf16),
             pltpu.VMEM((2, tokens // BLOCK, tokens), f32),
@@ -464,6 +651,12 @@
             pltpu.VMEM((dp, tokens, head), bf16),
             pltpu.VMEM((tokens, feats), bf16),
             pltpu.VMEM(ow.shape, bf16),
+            pltpu.VMEM((dp // 2 * feats, columns), bf16),
+            pltpu.VMEM((tokens, columns), bf16),
+            pltpu.VMEM((tokens, columns), bf16),
+            pltpu.VMEM((CHUNKS, 8, tokens // CHUNKS), f32),
+            pltpu.VMEM((CHUNKS, 8, tokens // CHUNKS), f32),
+            pltpu.VMEM((tokens, 1), f32),
             dma((3, dp, CHUNKS)),
             dma((dp, CHUNKS)),
             dma((dp // 2,)),
@@ -478,6 +671,10 @@
             dma((dp, CHUNKS)),
             dma((2,)),
             dma((2,)),
+            dma((dp // 2,)),
+            dma((dp // 2,)),
+            dma((2, CHUNKS)),
+            dma((2, CHUNKS)),
             dma((2,)),
         ],
         compiler_params=pltpu.CompilerParams(

time: 134 us -> 148 us (1.10)
  Pallas kernels: 130 us -> 143 us
    pallas_call x1, Pallas kernels: 130 us -> 143 us  [relay(): pl.pallas_call(functools.partial(relay_kernel, nz), out_shape=jax.ShapeDt...]
where the time goes in v2:
time: 148 us; the launch traced here: 147 us
  Pallas kernels  143 us (97%)
  local copies, waits for them, and re-layouts  3.84 us (3%)
    pallas_call x1, Pallas kernels, relay(): pl.pallas_call(functools.partial(relay_kernel, nz), out_shape=jax.ShapeDt...  143 us

profile of v2, /device:TPU:1, one launch (start us, length us, event | category | flops | bytes accessed | tf_op | source)
XLA Modules:
  0.0 147.3 jit_solution(3914916575042405564)
XLA Ops:
  0.0 1.4 copy.8
  1.4 143.5 %relay_layer.1 = bf16[1024,640]{1,0:T(8,128)(2,1)} custom-call(bf16[1024,640]{1,0:T(8,128)(2,1)} %bitcast.7, bf16[1,640]{1,0:T(2,128)(2,1)} %gain_ref.1, bf16[2560,384]{1,0:T(8,128)(2,1)} %bitcast.6, bf16[1024,640]{1,0:T(8,128)(2,1)} %bitcast.8, s32[16,3]{1,0:T(8,128)} %bitcast.9, s32[1,2]{1,0:T(1,128)} %glob_ref.1), custom_call_target="tpu_custom_call" | custom-call | tf_op jit(solution)/shard_map/relay_layer/pallas_call | solution.py:634
  144.8 2.5 %copy.10 = bf16[1,1024,640]{2,1,0:T(8,128)(2,1)} copy(bf16[1,1024,640]{2,1,0:T(8,128)(2,1)} %bitcast.5) | data formatting | bytes 2621440

commit v3 on v2

--- a/solution.py
+++ b/solution.py
@@ -117,6 +117,7 @@
     ss_out,
     ss_in,
     total_s,
+    rand_s,
     xs,
     xr,
     ws,
@@ -175,6 +176,8 @@
     own_w = pltpu.make_async_copy(
         w_ref, w_all.at[pl.ds(pl.multiple_of(y * half * feats, feats), half * feats), :], local.at[1]
     )
+    rand_copy = pltpu.make_async_copy(rand_ref, rand_s, local.at[2])
+    rand_copy.start()
     own_x.start()
     own_w.start()
     g_all[p] = jnp.broadcast_to(gain_ref[...].astype(jnp.float32), (8, feats))
@@ -288,7 +291,6 @@
             far_from_end(j).start()
             w_copy(quarter + j).start()
         for k in range(CHUNKS):
-            xhop(0, p, k, True).start()
             xhop(2, p, k, True).start()
 
     @pl.when(is_end & in_near)
@@ -309,6 +311,8 @@
     next_w.start()
 
     acc[...] = jnp.zeros_like(acc)
+
+    rand_copy.wait()
 
     blocks = tokens // BLOCK
     for h in range(2):
@@ -320,8 +324,8 @@
         for g in range(glob_ref.shape[1]):
             number = glob_ref[:, g : g + 1]
             allowed = allowed | (key_id == number) | (query_id == number)
-        for r in range(rand_ref.shape[1]):
-            allowed = allowed | (key_id == rand_ref[:, r : r + 1])
+        for r in range(rand_ref.shape[2]):
+            allowed = allowed | (key_id == rand_s[0, :, r : r + 1])
         bias[h] = jnp.where(allowed, 0.0, -jnp.inf)
 
     def scaled(b, k):
@@ -403,6 +407,13 @@
 
     @pl.when(is_end)
     def _():
+        @pl.when(in_far)
+        def _():
+            for j in range(quarter):
+                far_from_end(j).wait_send()
+            for k in range(CHUNKS):
+                xhop(0, p, k, True).start()
+
         @pl.when(in_near)
         def _():
             for j in range(quarter):
@@ -442,34 +453,22 @@
             far_shared(j).wait_recv()
             far_shared(j).start()
 
-        def rest_of_w():
-            for j in range(quarter):
-                w_copy(rest_w + j).start()
-
-        @pl.when(in_far)
-        def _():
-            arrived(mate, 0, 2)
-            share(0)
-            arrived(mate, 1, 2)
-            arrived(mate, 2, 2)
-            share(1)
-            rest_of_w()
-            arrived(mate, 3, 2)
-            arrived(end, 0, 0, 2)
-            arrived(end, 1, 0, 2)
-
-        @pl.when(in_near)
-        def _():
-            arrived(mate, 0, 2)
-            arrived(end, 0, 0, 2)
-            arrived(mate, 1, 2)
-            arrived(end, 1, 0, 2)
-            arrived(mate, 2, 2)
-            share(2)
-            arrived(mate, 3, 2)
-            rest_of_w()
-            arrived(end, 2, 0, 2)
-            share(3)
+        def when_far(fn):
+            pl.when(in_far)(fn)
+
+        def when_near(fn):
+            pl.when(in_near)(fn)
+
+        arrived(mate, 0, 2)
+        when_near(lambda: arrived(end, 0, 0, 2))
+        when_far(lambda: share(0))
+        arrived(mate, 1, 2)
+        when_near(lambda: arrived(end, 1, 0, 2))
+        arrived(mate, 2, 2)
+        when_far(lambda: share(1))
+        when_near(lambda: share(2))
+        arrived(mate, 3, 2)
+        when_far(lambda: arrived(end, 0, 0, 2))
 
         own_x.wait()
         own_w.wait()
@@ -479,8 +478,26 @@
         for k in range(CHUNKS):
             from_sib(sib, k)
             from_sib(other(mate), k)
-        for b in (p, sib, mate, other(mate)):
-            project_whole(b)
+        project_whole(p)
+        project_whole(sib)
+        when_far(lambda: arrived(end, 1, 0, 2))
+        when_near(lambda: share(3))
+        project_whole(mate)
+        project_whole(other(mate))
+        arrived(end, 2, 0, 2)
+
+        @pl.when(in_far)
+        def _():
+            for j in range(quarter):
+                far_shared(j).wait_send()
+
+        @pl.when(in_near)
+        def _():
+            for j in range(quarter, half):
+                far_shared(j).wait_send()
+
+        for j in range(quarter):
+            w_copy(rest_w + j).start()
 
         held = jnp.where(near == y, end, far_end)
         missing = jnp.where(near == y, far_end, end)
@@ -492,11 +509,6 @@
 
         for k in range(CHUNKS):
             if k == 2:
-                @pl.when(in_far)
-                def _():
-                    arrived(end, 2, 0, 2)
-
-            if k == 3:
                 arrived(end, 3, 0, 2)
             arrived(far_end, k, 2)
             if k > 0:
@@ -611,13 +623,9 @@
         def _():
             w_copy(j).wait_send()
 
-        @pl.when(in_far)
-        def _():
-            far_shared(j).wait_send()
-
-        @pl.when(in_near)
-        def _():
-            far_shared(quarter + j).wait_send()
+        @pl.when(is_end & in_near)
+        def _():
+            far_passed(quarter + j).wait_send()
 
     next_x.wait_send()
     next_w.wait_send()
@@ -634,7 +642,7 @@
     return pl.pallas_call(
         functools.partial(relay_kernel, nz),
         out_shape=jax.ShapeDtypeStruct((tokens, feats), bf16),
-        in_specs=[anywhere, vmem, anywhere, anywhere, vmem, vmem],
+        in_specs=[anywhere, vmem, anywhere, anywhere, anywhere, vmem],
         out_specs=vmem,
         scratch_shapes=[
             pltpu.VMEM((dp, tokens, feats), bf16),
@@ -657,6 +665,7 @@
             pltpu.VMEM((CHUNKS, 8, tokens // CHUNKS), f32),
             pltpu.VMEM((CHUNKS, 8, tokens // CHUNKS), f32),
             pltpu.VMEM((tokens, 1), f32),
+            pltpu.VMEM(rand.shape, jnp.int32),
             dma((3, dp, CHUNKS)),
             dma((dp, CHUNKS)),
             dma((dp // 2,)),
@@ -675,7 +684,7 @@
             dma((dp // 2,)),
             dma((2, CHUNKS)),
             dma((2, CHUNKS)),
-            dma((2,)),
+            dma((3,)),
         ],
         compiler_params=pltpu.CompilerParams(
             collective_id=0, has_side_effects=True, vmem_limit_bytes=56 * 1024 * 1024
@@ -712,7 +721,7 @@
             return shards(*args)
         out = relay(
             mesh.shape["dp"], section_input[0], norm_gain, qkv_weight[0], out_weight[0],
-            random_blocks[0], global_blocks,
+            random_blocks, global_blocks,
         )
         return out[None]
 

time: 148 us -> 129 us (0.87)
  Pallas kernels: 143 us -> 125 us
    pallas_call x1, Pallas kernels: 143 us -> 125 us  [relay(): pl.pallas_call(functools.partial(relay_kernel, nz), out_shape=jax.ShapeDt...]
    unnamed x1 -> x2, local copies, waits for them, and re-layouts: 2.49 us -> 3.84 us
where the time goes in v3:
time: 129 us
  Pallas kernels  125 us (97%)
  local copies, waits for them, and re-layouts  3.84 us (3%)
    pallas_call x1, Pallas kernels, relay(): pl.pallas_call(functools.partial(relay_kernel, nz), out_shape=jax.ShapeDt...  125 us
    unnamed x2, local copies, waits for them, and re-layouts  3.84 us

profile of v3, /device:TPU:1, one launch (start us, length us, event | category | flops | bytes accessed | tf_op | source)
XLA Modules:
  0.0 128.7 jit_solution(9508232422628472231)
XLA Ops:
  0.0 1.4 %copy.7.rand_ref = s32[1,16,3]{2,1,0:T(8,128)} copy(s32[1,16,3]{1,0,2:T(1,128)} %param.10) | data formatting | bytes 384 | tf_op args[4]
  1.4 124.9 %relay_layer.1 = bf16[1024,640]{1,0:T(8,128)(2,1)} custom-call(bf16[1024,640]{1,0:T(8,128)(2,1)} %bitcast.6, bf16[1,640]{1,0:T(2,128)(2,1)} %gain_ref.1, bf16[2560,384]{1,0:T(8,128)(2,1)} %bitcast.5, bf16[1024,640]{1,0:T(8,128)(2,1)} %bitcast.7, s32[1,16,3]{2,1,0:T(8,128)} %copy.7.rand_ref, s32[1,2]{1,0:T(1,128)} %glob_ref.1), custom_call_target="tpu_custom_call" | custom-call | tf_op jit(solution)/shard_map/relay_layer/pallas_call | solution.py:642
  126.2 2.5 %copy.9 = bf16[1,1024,640]{2,1,0:T(8,128)(2,1)} copy(bf16[1,1024,640]{2,1,0:T(8,128)(2,1)} %bitcast.4) | data formatting | bytes 2621440

commit v4 on v3

--- a/solution.py
+++ b/solution.py
@@ -287,16 +287,14 @@
 
     @pl.when(is_end & in_far)
     def _():
-        for j in range(quarter):
-            far_from_end(j).start()
-            w_copy(quarter + j).start()
+        far_from_end(0).start()
+        w_copy(quarter).start()
         for k in range(CHUNKS):
             xhop(2, p, k, True).start()
 
     @pl.when(is_end & in_near)
     def _():
-        for k in range(CHUNKS // 2):
-            xhop(0, p, k, True).start()
+        xhop(0, p, 0, True).start()
         for k in range(CHUNKS):
             xhop(2, p, k, True).start()
         for j in range(half):
@@ -337,11 +335,13 @@
         )
 
     def project_whole(b):
-        def body(k, _):
-            project(b, k)
+        def body(i, _):
+            at = pl.ds(pl.multiple_of(i * 2 * rows, 2 * rows), 2 * rows)
+            xg = (x_all[b, at, :].astype(jnp.float32) * g_all[b, 0:1, :]).astype(jnp.bfloat16)
+            acc[at, :] += jnp.dot(xg, w_all[rows_of(b), :], preferred_element_type=jnp.float32)
             return 0
 
-        lax.fori_loop(0, CHUNKS, body, 0)
+        lax.fori_loop(0, CHUNKS // 2, body, 0)
 
     def from_sib(b, k):
         xhop(2, b, k).wait_recv()
@@ -409,21 +409,39 @@
     def _():
         @pl.when(in_far)
         def _():
-            for j in range(quarter):
-                far_from_end(j).wait_send()
-            for k in range(CHUNKS):
-                xhop(0, p, k, True).start()
+            for j in range(1, quarter):
+                far_from_end(j - 1).wait_send()
+                far_from_end(j).start()
+                w_copy(quarter + j - 1).wait_send()
+                w_copy(quarter + j).start()
+            far_from_end(quarter - 1).wait_send()
+            xhop(0, p, 0, True).start()
 
         @pl.when(in_near)
         def _():
-            for j in range(quarter):
-                w_copy(quarter + j).wait_recv()
-                far_passed(quarter + j).start()
-                for k in range(CHUNKS // 2 + j, CHUNKS, quarter):
-                    xhop(0, p, k, True).start()
+            w_copy(quarter).wait_recv()
+            xhop(0, p, 0, True).wait_send()
+            far_passed(quarter).start()
+            for j in range(quarter + 1, half):
+                w_copy(j).wait_recv()
+                far_passed(j - 1).wait_send()
+                far_passed(j).start()
 
         for k in range(CHUNKS):
             arrived(mate, k, 2)
+
+        @pl.when(in_far)
+        def _():
+            xhop(0, p, 0, True).wait_send()
+
+        @pl.when(in_near)
+        def _():
+            far_passed(half - 1).wait_send()
+
+        for k in range(1, CHUNKS):
+            xhop(0, p, k, True).start()
+            if k < CHUNKS - 1:
+                xhop(0, p, k, True).wait_send()
         own_x.wait()
         own_w.wait()
         all_gains()
@@ -459,16 +477,14 @@
         def when_near(fn):
             pl.when(in_near)(fn)
 
-        arrived(mate, 0, 2)
         when_near(lambda: arrived(end, 0, 0, 2))
         when_far(lambda: share(0))
-        arrived(mate, 1, 2)
-        when_near(lambda: arrived(end, 1, 0, 2))
-        arrived(mate, 2, 2)
         when_far(lambda: share(1))
         when_near(lambda: share(2))
-        arrived(mate, 3, 2)
+        for k in range(CHUNKS):
+            arrived(mate, k, 2)
         when_far(lambda: arrived(end, 0, 0, 2))
+        when_near(lambda: share(3))
 
         own_x.wait()
         own_w.wait()
@@ -480,8 +496,7 @@
             from_sib(other(mate), k)
         project_whole(p)
         project_whole(sib)
-        when_far(lambda: arrived(end, 1, 0, 2))
-        when_near(lambda: share(3))
+        arrived(end, 1, 0, 2)
         project_whole(mate)
         project_whole(other(mate))
         arrived(end, 2, 0, 2)
@@ -602,11 +617,11 @@
         kv_copy(k).wait_send()
         att_copy(k).wait_send()
         xhop(2, p, k, True).wait_send()
-        xhop(0, p, k, True).wait_send()
         xhop(2, mate, k).wait_send()
 
         @pl.when(is_helper)
         def _():
+            xhop(0, p, k, True).wait_send()
             xhop(1, p, k, True).wait_send()
             xhop(0, end, k).wait_send()
             xhop(2, end, k).wait_send()
@@ -616,16 +631,18 @@
 
     for step in range(1, dp):
         gain_copy(lax.rem(p + step, dp), p).wait_send()
-    for j in range(quarter):
-        w_copy(quarter + j).wait_send()
-
-        @pl.when(jnp.logical_not(is_end & in_far))
-        def _():
+    @pl.when(is_end)
+    def _():
+        xhop(0, p, CHUNKS - 1, True).wait_send()
+
+    @pl.when(is_end & in_far)
+    def _():
+        w_copy(half - 1).wait_send()
+
+    @pl.when(jnp.logical_not(is_end & in_far))
+    def _():
+        for j in range(half):
             w_copy(j).wait_send()
-
-        @pl.when(is_end & in_near)
-        def _():
-            far_passed(quarter + j).wait_send()
 
     next_x.wait_send()
     next_w.wait_send()

time: 129 us -> 119 us (0.922)
  Pallas kernels: 125 us -> 115 us
    pallas_call x1, Pallas kernels: 125 us -> 115 us  [relay(): pl.pallas_call(functools.partial(relay_kernel, nz), out_shape=jax.ShapeDt...]
where the time goes in v4:
time: 119 us
  Pallas kernels  115 us (97%)
  local copies, waits for them, and re-layouts  3.84 us (3%)
    pallas_call x1, Pallas kernels, relay(): pl.pallas_call(functools.partial(relay_kernel, nz), out_shape=jax.ShapeDt...  115 us
    unnamed x2, local copies, waits for them, and re-layouts  3.84 us

profile of v4, /device:TPU:1, one launch (start us, length us, event | category | flops | bytes accessed | tf_op | source)
XLA Modules:
  0.0 118.7 jit_solution(15305429847959652332)
XLA Ops:
  0.0 1.4 %copy.7.rand_ref = s32[1,16,3]{2,1,0:T(8,128)} copy(s32[1,16,3]{1,0,2:T(1,128)} %param.10) | data formatting | bytes 384 | tf_op args[4]
  1.4 114.9 %relay_layer.1 = bf16[1024,640]{1,0:T(8,128)(2,1)} custom-call(bf16[1024,640]{1,0:T(8,128)(2,1)} %bitcast.6, bf16[1,640]{1,0:T(2,128)(2,1)} %gain_ref.1, bf16[2560,384]{1,0:T(8,128)(2,1)} %bitcast.5, bf16[1024,640]{1,0:T(8,128)(2,1)} %bitcast.7, s32[1,16,3]{2,1,0:T(8,128)} %copy.7.rand_ref, s32[1,2]{1,0:T(1,128)} %glob_ref.1), custom_call_target="tpu_custom_call" | custom-call | tf_op jit(solution)/shard_map/relay_layer/pallas_call | solution.py:659
  116.2 2.5 %copy.9 = bf16[1,1024,640]{2,1,0:T(8,128)(2,1)} copy(bf16[1,1024,640]{2,1,0:T(8,128)(2,1)} %bitcast.4) | data formatting | bytes 2621440

commit v5 on v4

--- a/solution.py
+++ b/solution.py
@@ -86,6 +86,7 @@
 
 
 CHUNKS = 4
+QUERIES = 8
 
 
 def relay_kernel(
@@ -169,6 +170,11 @@
     def part(k):
         return pl.ds(k * rows, rows)
 
+    few = tokens // QUERIES
+
+    def apart(k):
+        return pl.ds(k * few, few)
+
     def chunk(k):
         return pl.ds(pl.multiple_of(k * rows, rows), rows)
 
@@ -185,7 +191,7 @@
     pl.semaphore_wait(barrier, dp + 1)
 
     def hop(buf, send, recv, way, b, k, src=None):
-        at = buf.at[b, part(k), :]
+        at = buf.at[b, apart(k), :]
         to = (p - 2, p + 2, sib)[way]
         return remote(at if src is None else src, at, send.at[way, b, k], recv.at[b, k], {"dp": to})
 
@@ -536,51 +542,49 @@
             project(other(missing), k)
             finish_joined(k, acc[part(k), :], total_s[part(k), :])
 
-    per = blocks // CHUNKS
+    per = blocks // QUERIES
 
     def scores_of(k, h):
         s = lax.dot_general(
-            q_s[part(k), :], kv[h, :, :head], (((1,), (1,)), ((), ())),
+            q_s[apart(k), :], kv[h, :, :head], (((1,), (1,)), ((), ())),
             preferred_element_type=jnp.float32,
         )
         s = (s * scale).reshape(per, BLOCK, tokens)
         s = s + bias[h, k * per : (k + 1) * per, :][:, None, :]
-        return s.reshape(rows, tokens)
+        return s.reshape(few, tokens)
 
     def own_keys(k):
         s = scores_of(k, 0)
         m = jnp.max(s, axis=1, keepdims=True)
         e = jnp.exp2(s - m)
-        m_s[part(k), :] = m
-        l_s[part(k), :] = jnp.sum(e, axis=1, keepdims=True)
-        o_s[part(k), :] = jnp.dot(
+        m_s[apart(k), :] = m
+        l_s[apart(k), :] = jnp.sum(e, axis=1, keepdims=True)
+        o_s[apart(k), :] = jnp.dot(
             e.astype(jnp.bfloat16), kv[0, :, head:], preferred_element_type=jnp.float32
         )
 
     def att_copy(k):
         return remote(
-            att_own.at[part(k), :], att_all.at[p, part(k), :], ts.at[k], ar.at[p, k], {"section": 1 - sec}
+            att_own.at[apart(k), :], att_all.at[p, apart(k), :], ts.at[k], ar.at[p, k], {"section": 1 - sec}
         )
 
     def other_keys(k):
         s = scores_of(k, 1)
-        before = m_s[part(k), :]
+        before = m_s[apart(k), :]
         m = jnp.maximum(before, jnp.max(s, axis=1, keepdims=True))
         e = jnp.exp2(s - m)
         shrink = jnp.exp2(before - m)
-        total = l_s[part(k), :] * shrink + jnp.sum(e, axis=1, keepdims=True)
-        o = o_s[part(k), :] * shrink + jnp.dot(
+        total = l_s[apart(k), :] * shrink + jnp.sum(e, axis=1, keepdims=True)
+        o = o_s[apart(k), :] * shrink + jnp.dot(
             e.astype(jnp.bfloat16), kv[1, :, head:], preferred_element_type=jnp.float32
         )
-        att_own[part(k), :] = (o / total).astype(jnp.bfloat16)
+        att_own[apart(k), :] = (o / total).astype(jnp.bfloat16)
         att_copy(k).start()
 
-    for k in range(CHUNKS):
+    for k in range(2):
         own_keys(k)
     for k in range(CHUNKS):
         kv_copy(k).wait_recv()
-    next_x.wait_recv()
-    next_w.wait_recv()
 
     def att_step(d, k):
         if d == 0:
@@ -589,7 +593,7 @@
         else:
             chain(att_all, as_, ar, d, k)
 
-    def finish(k):
+    def gathered(k):
         hop(att_all, as_, ar, 2, sib, k).wait_recv()
         for d in range(1, nz):
             @pl.when(z + d < nz)
@@ -599,23 +603,36 @@
             @pl.when(z - d >= 0)
             def _():
                 hop(att_all, as_, ar, 2, sib - 2 * d, k).wait_recv()
-        heads = jnp.concatenate([att_all[b, part(k), :] for b in range(dp)], axis=1)
+
+    def finish(k):
+        at = part(k)
+        heads = jnp.concatenate([att_all[b, at, :] for b in range(dp)], axis=1)
         added = jnp.dot(heads, ow_next[...], preferred_element_type=jnp.float32)
-        out_ref[part(k), :] = (x_next[part(k), :].astype(jnp.float32) + added).astype(jnp.bfloat16)
-
-    for i in range(CHUNKS + nz + 1):
-        if i < CHUNKS:
+        out_ref[at, :] = (x_next[at, :].astype(jnp.float32) + added).astype(jnp.bfloat16)
+
+    split = QUERIES // CHUNKS
+    for i in range(QUERIES + nz + 1):
+        if i < QUERIES:
             other_keys(i)
+            if i + 2 < QUERIES:
+                own_keys(i + 2)
         for d in range(nz):
-            if 0 <= i - 1 - d < CHUNKS:
+            if 0 <= i - 1 - d < QUERIES:
                 att_step(d, i - 1 - d)
-        if 0 <= i - nz - 1 < CHUNKS:
-            finish(i - nz - 1)
-
+        done = i - nz - 1
+        if done == 0:
+            next_x.wait_recv()
+            next_w.wait_recv()
+        if 0 <= done < QUERIES:
+            gathered(done)
+            if done % split == split - 1:
+                finish(done // split)
+
+    for k in range(QUERIES):
+        drain(att_all, as_, ar, k)
+        att_copy(k).wait_send()
     for k in range(CHUNKS):
-        drain(att_all, as_, ar, k)
         kv_copy(k).wait_send()
-        att_copy(k).wait_send()
         xhop(2, p, k, True).wait_send()
         xhop(2, mate, k).wait_send()
 
@@ -691,10 +708,10 @@
             dma((dp,)),
             dma((CHUNKS,)),
             dma((CHUNKS,)),
-            dma((CHUNKS,)),
-            dma((CHUNKS,)),
-            dma((3, dp, CHUNKS)),
-            dma((dp, CHUNKS)),
+            dma((QUERIES,)),
+            dma((QUERIES,)),
+            dma((3, dp, QUERIES)),
+            dma((dp, QUERIES)),
             dma((2,)),
             dma((2,)),
             dma((dp // 2,)),
@@ -717,7 +734,7 @@
         and mesh.shape["dp"] == 8
         and feats % 128 == 0
         and columns % 384 == 0
-        and tokens % (CHUNKS * BLOCK) == 0
+        and tokens % (QUERIES * BLOCK) == 0
     )
 
 

time: 119 us -> 128 us (1.076)
  Pallas kernels: 115 us -> 124 us
    pallas_call x1, Pallas kernels: 115 us -> 124 us  [relay(): pl.pallas_call(functools.partial(relay_kernel, nz), out_shape=jax.ShapeDt...]
where the time goes in v5:
time: 128 us
  Pallas kernels  124 us (97%)
  local copies, waits for them, and re-layouts  3.84 us (3%)
    pallas_call x1, Pallas kernels, relay(): pl.pallas_call(functools.partial(relay_kernel, nz), out_shape=jax.ShapeDt...  124 us
    unnamed x2, local copies, waits for them, and re-layouts  3.84 us

profile of v5, /device:TPU:1, one launch (start us, length us, event | category | flops | bytes accessed | tf_op | source)
XLA Modules:
  0.0 127.8 jit_solution(12000778088227785709)
XLA Ops:
  0.0 1.4 %copy.7.rand_ref = s32[1,16,3]{2,1,0:T(8,128)} copy(s32[1,16,3]{1,0,2:T(1,128)} %param.10) | data formatting | bytes 384 | tf_op args[4]
  1.4 124.0 %relay_layer.1 = bf16[1024,640]{1,0:T(8,128)(2,1)} custom-call(bf16[1024,640]{1,0:T(8,128)(2,1)} %bitcast.6, bf16[1,640]{1,0:T(2,128)(2,1)} %gain_ref.1, bf16[2560,384]{1,0:T(8,128)(2,1)} %bitcast.5, bf16[1024,640]{1,0:T(8,128)(2,1)} %bitcast.7, s32[1,16,3]{2,1,0:T(8,128)} %copy.7.rand_ref, s32[1,2]{1,0:T(1,128)} %glob_ref.1), custom_call_target="tpu_custom_call" | custom-call | tf_op jit(solution)/shard_map/relay_layer/pallas_call | solution.py:676
  125.3 2.5 %copy.9 = bf16[1,1024,640]{2,1,0:T(8,128)(2,1)} copy(bf16[1,1024,640]{2,1,0:T(8,128)(2,1)} %bitcast.4) | data formatting | bytes 2621440

commit v6 on v4

--- a/solution.py
+++ b/solution.py
@@ -538,22 +538,23 @@
 
     per = blocks // CHUNKS
 
-    def scores_of(k, h):
+    def scores_of(k, h, count):
         s = lax.dot_general(
-            q_s[part(k), :], kv[h, :, :head], (((1,), (1,)), ((), ())),
+            q_s[pl.ds(k * rows, count * rows), :], kv[h, :, :head], (((1,), (1,)), ((), ())),
             preferred_element_type=jnp.float32,
         )
-        s = (s * scale).reshape(per, BLOCK, tokens)
-        s = s + bias[h, k * per : (k + 1) * per, :][:, None, :]
-        return s.reshape(rows, tokens)
-
-    def own_keys(k):
-        s = scores_of(k, 0)
+        s = (s * scale).reshape(count * per, BLOCK, tokens)
+        s = s + bias[h, k * per : (k + count) * per, :][:, None, :]
+        return s.reshape(count * rows, tokens)
+
+    def own_keys(k, count):
+        at = pl.ds(k * rows, count * rows)
+        s = scores_of(k, 0, count)
         m = jnp.max(s, axis=1, keepdims=True)
         e = jnp.exp2(s - m)
-        m_s[part(k), :] = m
-        l_s[part(k), :] = jnp.sum(e, axis=1, keepdims=True)
-        o_s[part(k), :] = jnp.dot(
+        m_s[at, :] = m
+        l_s[at, :] = jnp.sum(e, axis=1, keepdims=True)
+        o_s[at, :] = jnp.dot(
             e.astype(jnp.bfloat16), kv[0, :, head:], preferred_element_type=jnp.float32
         )
 
@@ -563,7 +564,7 @@
         )
 
     def other_keys(k):
-        s = scores_of(k, 1)
+        s = scores_of(k, 1, 1)
         before = m_s[part(k), :]
         m = jnp.maximum(before, jnp.max(s, axis=1, keepdims=True))
         e = jnp.exp2(s - m)
@@ -575,12 +576,9 @@
         att_own[part(k), :] = (o / total).astype(jnp.bfloat16)
         att_copy(k).start()
 
-    for k in range(CHUNKS):
-        own_keys(k)
+    own_keys(0, CHUNKS // 2)
     for k in range(CHUNKS):
         kv_copy(k).wait_recv()
-    next_x.wait_recv()
-    next_w.wait_recv()
 
     def att_step(d, k):
         if d == 0:
@@ -606,9 +604,14 @@
     for i in range(CHUNKS + nz + 1):
         if i < CHUNKS:
             other_keys(i)
+        if i == CHUNKS // 2 - 1:
+            own_keys(CHUNKS // 2, CHUNKS // 2)
         for d in range(nz):
             if 0 <= i - 1 - d < CHUNKS:
                 att_step(d, i - 1 - d)
+        if i == nz + 1:
+            next_x.wait_recv()
+            next_w.wait_recv()
         if 0 <= i - nz - 1 < CHUNKS:
             finish(i - nz - 1)
 

time: 119 us -> 119 us (level)
  no operation moved by 1% of the time
where the time goes in v6:
time: 119 us
  Pallas kernels  115 us (97%)
  local copies, waits for them, and re-layouts  3.84 us (3%)
    pallas_call x1, Pallas kernels, relay(): pl.pallas_call(functools.partial(relay_kernel, nz), out_shape=jax.ShapeDt...  115 us
    unnamed x2, local copies, waits for them, and re-layouts  3.84 us

profile of v6, /device:TPU:1, one launch (start us, length us, event | category | flops | bytes accessed | tf_op | source)
XLA Modules:
  0.0 118.9 jit_solution(12429050163056759941)
XLA Ops:
  0.0 1.4 %copy.7.rand_ref = s32[1,16,3]{2,1,0:T(8,128)} copy(s32[1,16,3]{1,0,2:T(1,128)} %param.10) | data formatting | bytes 384 | tf_op args[4]
  1.4 115.1 %relay_layer.1 = bf16[1024,640]{1,0:T(8,128)(2,1)} custom-call(bf16[1024,640]{1,0:T(8,128)(2,1)} %bitcast.6, bf16[1,640]{1,0:T(2,128)(2,1)} %gain_ref.1, bf16[2560,384]{1,0:T(8,128)(2,1)} %bitcast.5, bf16[1024,640]{1,0:T(8,128)(2,1)} %bitcast.7, s32[1,16,3]{2,1,0:T(8,128)} %copy.7.rand_ref, s32[1,2]{1,0:T(1,128)} %glob_ref.1), custom_call_target="tpu_custom_call" | custom-call | tf_op jit(solution)/shard_map/relay_layer/pallas_call | solution.py:662
  116.4 2.5 %copy.9 = bf16[1,1024,640]{2,1,0:T(8,128)(2,1)} copy(bf16[1,1024,640]{2,1,0:T(8,128)(2,1)} %bitcast.4) | data formatting | bytes 2621440

commit v7 on v4

--- a/solution.py
+++ b/solution.py
@@ -499,7 +499,6 @@
         arrived(end, 1, 0, 2)
         project_whole(mate)
         project_whole(other(mate))
-        arrived(end, 2, 0, 2)
 
         @pl.when(in_far)
         def _():
@@ -513,6 +512,7 @@
 
         for j in range(quarter):
             w_copy(rest_w + j).start()
+        arrived(end, 2, 0, 2)
 
         held = jnp.where(near == y, end, far_end)
         missing = jnp.where(near == y, far_end, end)

time: 119 us -> 118 us (level)
  no operation moved by 1% of the time
where the time goes in v7:
time: 118 us
  Pallas kernels  114 us (97%)
  local copies, waits for them, and re-layouts  3.84 us (3%)
    pallas_call x1, Pallas kernels, relay(): pl.pallas_call(functools.partial(relay_kernel, nz), out_shape=jax.ShapeDt...  114 us
    unnamed x2, local copies, waits for them, and re-layouts  3.84 us

profile of v7, /device:TPU:1, one launch (start us, length us, event | category | flops | bytes accessed | tf_op | source)
XLA Modules:
  0.0 117.5 jit_solution(17489824497953368281)
XLA Ops:
  0.0 1.4 %copy.7.rand_ref = s32[1,16,3]{2,1,0:T(8,128)} copy(s32[1,16,3]{1,0,2:T(1,128)} %param.10) | data formatting | bytes 384 | tf_op args[4]
  1.4 113.7 %relay_layer.1 = bf16[1024,640]{1,0:T(8,128)(2,1)} custom-call(bf16[1024,640]{1,0:T(8,128)(2,1)} %bitcast.6, bf16[1,640]{1,0:T(2,128)(2,1)} %gain_ref.1, bf16[2560,384]{1,0:T(8,128)(2,1)} %bitcast.5, bf16[1024,640]{1,0:T(8,128)(2,1)} %bitcast.7, s32[1,16,3]{2,1,0:T(8,128)} %copy.7.rand_ref, s32[1,2]{1,0:T(1,128)} %glob_ref.1), custom_call_target="tpu_custom_call" | custom-call | tf_op jit(solution)/shard_map/relay_layer/pallas_call | solution.py:659
  115.1 2.5 %copy.9 = bf16[1,1024,640]{2,1,0:T(8,128)(2,1)} copy(bf16[1,1024,640]{2,1,0:T(8,128)(2,1)} %bitcast.4) | data formatting | bytes 2621440
